TPU v7x, 256 devices: a whole 4x4x8 slice. The times are simulated.
256 devices in a mesh: gx: 16 (over z, y_lo), gy: 8 (over x, y_hi), gz: 2 (over core).
Axes of the slice: x: 4, y: 4 (y_hi: 2, y_lo: 2; y = y_hi * 2 + y_lo), z: 8, core: 2. Of those that a mesh axis runs over, the one named last changes fastest.
Arguments:
- toroidal: float32 [2, 2, 2048, 2048], P(None, 'gz', 'gx', 'gy'), may hold values from -6 to 6
- poloidal: float32 [2, 2, 2048, 2048], P(None, 'gz', 'gx', 'gy'), may hold values from -6 to 6
Outputs:
- velocity: float32 [3, 2, 2, 2048, 2048], P(None, None, 'gz', 'gx', 'gy')
All inputs are finite; a program needn't handle non-finite values.
Results may differ from a plain program's by a relative error of at most 0.0001.
Values sent between devices are 32-bit elements; how exact they have to be, the bound alone decides.
No kernel may reach another device: no remote copies, remote signals or barrier semaphores. Data moves between devices by JAX's collectives and lax.ppermute only.
A program may use at most 64 MiB of HBM per device.

v0:
```python
import math

import jax
import jax.numpy as jnp
from jax import lax
from jax.sharding import PartitionSpec as P

NX = 2048
KZ_FIRST = 128
K0 = 512


def swapped(value, axis, apart):
    mask = 2**apart
    pairs = [(source, source ^ mask) for source in range(lax.axis_size(axis))]
    return lax.ppermute(value, axis, pairs)


def velocity_spectrum(toroidal, poloidal, wave_x, wave_y, wave_z):
    horiz = wave_x * wave_x + wave_y * wave_y
    square = horiz + wave_z * wave_z
    magnitude = jnp.sqrt(square)
    ratio = square / (K0 * K0)
    shaping = 4.0 / NX * ratio * jnp.exp(1.0 - ratio)
    tor_gain = shaping / magnitude
    pol_gain = shaping / square
    tor_re, tor_im = (toroidal[0], toroidal[1])
    pol_re, pol_im = (poloidal[0], poloidal[1])
    cross = wave_z * pol_gain
    first_re = -wave_y * tor_gain * tor_im - wave_x * cross * pol_re
    first_im = wave_y * tor_gain * tor_re - wave_x * cross * pol_im
    second_re = wave_x * tor_gain * tor_im - wave_y * cross * pol_re
    second_im = -wave_x * tor_gain * tor_re - wave_y * cross * pol_im
    third_re = horiz * pol_gain * pol_re
    third_im = horiz * pol_gain * pol_im
    return jnp.stack(
        [
            jnp.stack([first_re, first_im]),
            jnp.stack([second_re, second_im]),
            jnp.stack([third_re, third_im]),
        ]
    )


def reverse_bits(values, nbits):
    result = jnp.zeros_like(values)
    for place in range(nbits):
        result = result + jnp.left_shift(
            jnp.bitwise_and(jnp.right_shift(values, place), 1), nbits - 1 - place
        )
    return result


def phase_table(phase, period):
    angle = phase.astype(jnp.float32) * (2.0 * math.pi / period)
    return (jnp.cos(angle), jnp.sin(angle))


def complex_apply(form, table_re, table_im, real_part, imag_part):
    high = lax.Precision.HIGHEST
    out_re = jnp.einsum(form, table_re, real_part, precision=high) - jnp.einsum(
        form, table_im, imag_part, precision=high
    )
    out_im = jnp.einsum(form, table_re, imag_part, precision=high) + jnp.einsum(
        form, table_im, real_part, precision=high
    )
    return jnp.stack([out_re, out_im], axis=1)


def along_rows(field, total, offset):
    rows = field.shape[3]
    parts = total // rows
    out_row = jnp.arange(rows, dtype=jnp.int32)[:, None]
    in_row = jnp.arange(rows, dtype=jnp.int32)[None, :]
    table_re, table_im = phase_table(in_row * (out_row * parts + offset) % total, total)
    return complex_apply("jm,ckmy->ckjy", table_re, table_im, field[:, 0], field[:, 1])


def signed_waves(glob, total):
    return jnp.where(glob < total // 2, glob, glob - total).astype(jnp.float32)


def local(toroidal, poloidal):
    planes = toroidal.shape[1]
    rows = toroidal.shape[2]
    cols = toroidal.shape[3]
    parts_x = lax.axis_size("gx")
    total_x = rows * parts_x
    total_y = cols * lax.axis_size("gy")
    index_x = lax.axis_index("gx")
    index_y = lax.axis_index("gy")
    index_z = lax.axis_index("gz")
    nbits = parts_x.bit_length() - 1
    wave_z = (KZ_FIRST + index_z * planes + jnp.arange(planes, dtype=jnp.int32)).astype(jnp.float32)
    residue = reverse_bits(index_x, nbits)
    glob_x = index_x * rows + jnp.arange(rows, dtype=jnp.int32)
    glob_y = index_y * cols + jnp.arange(cols, dtype=jnp.int32)
    field = velocity_spectrum(
        toroidal,
        poloidal,
        signed_waves(glob_x, total_x)[None, :, None],
        signed_waves(glob_y, total_y)[None, None, :],
        wave_z[:, None, None],
    )
    for place in reversed(range(nbits)):
        partner = swapped(field, "gx", place)
        half = 1 << place
        upper = jnp.bitwise_and(jnp.right_shift(index_x, place), 1) == 1
        rot_cos, rot_sin = phase_table(index_x % half * (parts_x // (2 * half)), parts_x)
        differ = partner - field
        rotated = jnp.stack(
            [
                differ[:, 0] * rot_cos - differ[:, 1] * rot_sin,
                differ[:, 0] * rot_sin + differ[:, 1] * rot_cos,
            ],
            axis=1,
        )
        field = jnp.where(upper, rotated, field + partner)
    field = along_rows(field, total_x, residue)
    block = lax.all_to_all(field, "gy", split_axis=3, concat_axis=4, tiled=True)
    lines = block.shape[4]
    outer = 2 ** ((lines.bit_length() - 1) // 2)
    inner = lines // outer
    shaped = block.reshape(block.shape[0], 2, block.shape[2], block.shape[3], outer, inner)
    first = jnp.arange(outer, dtype=jnp.int32)
    second = jnp.arange(inner, dtype=jnp.int32)
    table_re, table_im = phase_table(first[:, None] * first[None, :] % outer, outer)
    section = complex_apply("qb,ckrba->ckrqa", table_re, table_im, shaped[:, 0], shaped[:, 1])
    twist_re, twist_im = phase_table(first[:, None] * second[None, :] % lines, lines)
    section = jnp.stack(
        [
            section[:, 0] * twist_re - section[:, 1] * twist_im,
            section[:, 0] * twist_im + section[:, 1] * twist_re,
        ],
        axis=1,
    )
    table_re, table_im = phase_table(second[:, None] * second[None, :] % inner, inner)
    final = complex_apply("na,ckrqa->ckrnq", table_re, table_im, section[:, 0], section[:, 1])
    final = final.reshape(block.shape[0], 2, block.shape[2], block.shape[3], lines)
    return lax.all_to_all(final, "gy", split_axis=4, concat_axis=3, tiled=True)


def solution(mesh):
    in_specs = (P(None, "gz", "gx", "gy"), P(None, "gz", "gx", "gy"))
    out_specs = P(None, None, "gz", "gx", "gy")
    return jax.shard_map(local, mesh=mesh, in_specs=in_specs, out_specs=out_specs, check_vma=False)
```

profile of v0, /device:TPU:8, one launch (start us, length us, event | category | flops | bytes accessed | tf_op | source)
XLA Modules:
  0.0 209.9 jit_solution(10315602289031182742)
XLA Ops:
  0.1 1.0 fusion.137
  1.1 1.0 fusion.138
  2.8 7.3 %collective-permute-start = (f32[3,2,1,128,256]{3,4,0,2,1:T(8,128)S(1)}, f32[3,2,1,128,256]{3,4,0,2,1:T(8,128)S(1)}, u32[]{:S(2)}, u32[]{:S(2)}) collective-permute-start(f32[3,2,1,128,256]{3,4,0,2,1:T(8,128)S(1)} %pad_maximum_fusion), channel_id=1, source_target_pairs={{0,128},{16,144},{32,160},{48,176},{64,192},{80,208},{96,224},{112... | collective-permute-start | bytes 2359304 | tf_op jit(solution)/shard_map/ppermute | solution.py:16
  10.3 32.9 %collective-permute-done = f32[3,2,1,128,256]{3,4,0,2,1:T(8,128)S(1)} collective-permute-done((f32[3,2,1,128,256]{3,4,0,2,1:T(8,128)S(1)}, f32[3,2,1,128,256]{3,4,0,2,1:T(8,128)S(1)}, u32[]{:S(2)}, u32[]{:S(2)}) %collective-permute-start) | collective-permute-done | bytes 786464 | tf_op jit(solution)/shard_map/ppermute | solution.py:16
  43.4 1.0 maximum_select_fusion
  44.4 3.1 %collective-permute-start.1 = (f32[3,2,1,128,256]{3,4,0,2,1:T(8,128)}, f32[3,2,1,128,256]{3,4,0,2,1:T(8,128)S(1)}, u32[]{:S(2)}, u32[]{:S(2)}) collective-permute-start(f32[3,2,1,128,256]{3,4,0,2,1:T(8,128)} %maximum_select_fusion), channel_id=1, source_target_pairs={{0,64},{16,80},{32,96},{48,112},{64,0},{80,16},{96,32},{112,48},{1... | collective-permute-start | bytes 2359304 | tf_op jit(solution)/shard_map/ppermute | solution.py:16
  47.6 33.9 %collective-permute-done.1 = f32[3,2,1,128,256]{3,4,0,2,1:T(8,128)S(1)} collective-permute-done((f32[3,2,1,128,256]{3,4,0,2,1:T(8,128)}, f32[3,2,1,128,256]{3,4,0,2,1:T(8,128)S(1)}, u32[]{:S(2)}, u32[]{:S(2)}) %collective-permute-start.1) | collective-permute-done | bytes 786464 | tf_op jit(solution)/shard_map/ppermute | solution.py:16
  82.5 1.4 maximum_select_fusion.1
  84.1 18.0 %collective-permute-done.2 = f32[3,2,1,128,256]{3,4,0,2,1:T(8,128)S(1)} collective-permute-done((f32[3,2,1,128,256]{3,4,0,2,1:T(8,128)S(1)}, f32[3,2,1,128,256]{3,4,0,2,1:T(8,128)S(1)}, u32[]{:S(2)}, u32[]{:S(2)}) %collective-permute-start.2) | collective-permute-done | bytes 786464 | tf_op jit(solution)/shard_map/ppermute | solution.py:16
  102.9 16.8 %collective-permute-done.3 = f32[3,2,1,128,256]{3,4,0,2,1:T(8,128)S(1)} collective-permute-done((f32[3,2,1,128,256]{3,4,0,2,1:T(8,128)S(1)}, f32[3,2,1,128,256]{3,4,0,2,1:T(8,128)S(1)}, u32[]{:S(2)}, u32[]{:S(2)}) %collective-permute-start.3) | collective-permute-done | bytes 786464 | tf_op jit(solution)/shard_map/ppermute | solution.py:16
  120.0 0.8 fusion.15
  120.7 0.8 fusion.14
  121.5 0.8 fusion.5
  122.3 0.8 fusion.4
  123.1 1.2 copy.55
  124.3 6.0 %all-to-all-start = ((f32[3,2,1,128,256]{4,1,2,0,3:T(2,128)}), f32[3,2,1,128,256]{4,1,2,0,3:T(2,128)S(1)}, u32[]{:S(2)}, u32[]{:S(2)}) async-start(f32[3,2,1,128,256]{4,1,2,0,3:T(2,128)} %copy.55), calls=%async_computation | async-start | bytes 1572864 | tf_op jit(solution)/shard_map/all_to_all | solution.py:120
  130.4 10.8 %all-to-all-done = f32[3,2,1,128,256]{4,1,2,0,3:T(2,128)S(1)} async-done(((f32[3,2,1,128,256]{4,1,2,0,3:T(2,128)}), f32[3,2,1,128,256]{4,1,2,0,3:T(2,128)S(1)}, u32[]{:S(2)}, u32[]{:S(2)}) %all-to-all-start) | async-done | bytes 786464 | tf_op jit(solution)/shard_map/all_to_all | solution.py:120
  142.0 0.9 fusion.12
  142.9 0.9 fusion.13
  143.8 0.9 fusion.3
  144.7 0.9 fusion.2
  145.6 0.9 fusion.10
  146.5 1.8 fusion.6
  148.3 1.8 fusion.1
  150.1 1.6 copy.58
  152.5 2.1 fusion
  155.8 6.6 %copy.60 = f32[3,2,1,16,2048]{3,1,2,0,4:T(2,128)} copy(f32[3,2,1,16,2048]{4,3,0,2,1:T(8,128)S(1)} %pad_maximum_fusion.2) | data formatting | bytes 1572864 | tf_op jit(solution)/shard_map/stack | solution.py:67
  162.4 10.0 %reshape.806 = f32[8,1,24576]{2,1,0:T(1,128)S(1)} reshape(f32[2048,3,1,2,16]{4,3,2,1,0:T(2,128)} %bitcast.126) | data formatting | bytes 1572864
  172.4 14.6 %all_to_all.33 = f32[8,1,24576]{2,1,0:T(1,128)S(1)} all-to-all(f32[8,1,24576]{2,1,0:T(1,128)S(1)} %reshape.806), channel_id=1, replica_groups=mesh['gx'=16,'gy'=8,'gz'=2] {'gy'}, dimensions={0} | all-to-all | bytes 1572864 | tf_op jit(solution)/shard_map/all_to_all | solution.py:140
  187.5 2.5 %reduce = f32[8,24576]{1,0:T(8,128)S(1)} reduce(f32[8,1,24576]{2,1,0:T(1,128)S(1)} %all_to_all.33, f32[]{:T(128)} %broadcast.836), dimensions={1}, to_apply=%all_to_all.27.reduce_sub_computation | reduce | bytes 1572868 | tf_op jit(solution)/shard_map/all_to_all | solution.py:140
  190.0 11.1 %reshape.807 = f32[2048,3,1,2,16]{4,3,2,1,0:T(2,128)} reshape(f32[8,24576]{1,0:T(8,128)S(1)} %reduce) | data formatting | bytes 1572864
  201.1 8.8 %copy.69 = f32[3,2,1,16,8,256]{5,3,4,1,0,2:T(8,128)} copy(f32[3,2,1,16,8,256]{3,1,0,5,4,2:T(2,128)} %bitcast.127) | data formatting | bytes 1572864 | tf_op jit(solution)/shard_map/all_to_all | solution.py:140
  (40 shorter events, 6.5 us)
Async XLA Ops:
  2.8 40.3 %collective-permute-start = (f32[3,2,1,128,256]{3,4,0,2,1:T(8,128)S(1)}, f32[3,2,1,128,256]{3,4,0,2,1:T(8,128)S(1)}, u32[]{:S(2)}, u32[]{:S(2)}) collective-permute-start(f32[3,2,1,128,256]{3,4,0,2,1:T(8,128)S(1)} %pad_maximum_fusion), channel_id=1, source_target_pairs={{0,128},{16,144},{32,160},{48,176},{64,192},{80,208},{96,224},{112... | collective-permute-start | bytes 2359304 | tf_op jit(solution)/shard_map/ppermute | solution.py:16
  44.4 37.2 %collective-permute-start.1 = (f32[3,2,1,128,256]{3,4,0,2,1:T(8,128)}, f32[3,2,1,128,256]{3,4,0,2,1:T(8,128)S(1)}, u32[]{:S(2)}, u32[]{:S(2)}) collective-permute-start(f32[3,2,1,128,256]{3,4,0,2,1:T(8,128)} %maximum_select_fusion), channel_id=1, source_target_pairs={{0,64},{16,80},{32,96},{48,112},{64,0},{80,16},{96,32},{112,48},{1... | collective-permute-start | bytes 2359304 | tf_op jit(solution)/shard_map/ppermute | solution.py:16
  81.5 0.9 copy-start
  83.9 18.2 %collective-permute-start.2 = (f32[3,2,1,128,256]{3,4,0,2,1:T(8,128)S(1)}, f32[3,2,1,128,256]{3,4,0,2,1:T(8,128)S(1)}, u32[]{:S(2)}, u32[]{:S(2)}) collective-permute-start(f32[3,2,1,128,256]{3,4,0,2,1:T(8,128)S(1)} %maximum_select_fusion.1), channel_id=1, source_target_pairs={{0,32},{16,48},{32,0},{48,16},{64,96},{80,112},{96,64},{112,80},{1... | collective-permute-start | bytes 2359304 | tf_op jit(solution)/shard_map/ppermute | solution.py:16
  102.4 17.3 %collective-permute-start.3 = (f32[3,2,1,128,256]{3,4,0,2,1:T(8,128)S(1)}, f32[3,2,1,128,256]{3,4,0,2,1:T(8,128)S(1)}, u32[]{:S(2)}, u32[]{:S(2)}) collective-permute-start(f32[3,2,1,128,256]{3,4,0,2,1:T(8,128)S(1)} %maximum_select_fusion.2), channel_id=1, source_target_pairs={{0,16},{16,0},{32,48},{48,32},{64,80},{80,64},{96,112},{112,96},{1... | collective-permute-start | bytes 2359304 | tf_op jit(solution)/shard_map/ppermute | solution.py:16
  124.3 16.9 %all-to-all-start = ((f32[3,2,1,128,256]{4,1,2,0,3:T(2,128)}), f32[3,2,1,128,256]{4,1,2,0,3:T(2,128)S(1)}, u32[]{:S(2)}, u32[]{:S(2)}) async-start(f32[3,2,1,128,256]{4,1,2,0,3:T(2,128)} %copy.55), calls=%async_computation | async-start | bytes 1572864 | tf_op jit(solution)/shard_map/all_to_all | solution.py:120
  130.4 17.9 %copy-start.1 = (f32[32,64]{1,0:T(8,128)}, f32[32,64]{1,0:T(8,128)S(1)}, u32[]{:S(2)}) copy-start(f32[32,64]{1,0:T(8,128)S(1)} %get-tuple-element.31) | copy-start | bytes 24580
where the time goes:
time: 210 us
  waiting for transfers between devices  112 us (53%)
  local copies, waits for them, and re-layouts  45.6 us (22%)
  starting transfers between devices  17 us (8%)
  blocking collectives  14.6 us (7%)
  matrix products  13.2 us (6%)
  other arithmetic  6.38 us (3%)
    ppermute x4, waiting for transfers between devices, swapped(): return lax.ppermute(value, axis, pairs)  102 us
    unnamed x10, local copies, waits for them, and re-layouts  22.2 us
    all_to_all x1, blocking collectives, local(): return lax.all_to_all(final, 'gy', split_axis=4, concat_axis=3, tiled=True)  14.6 us
    ppermute x4, starting transfers between devices, swapped(): return lax.ppermute(value, axis, pairs)  11 us
    all_to_all x1, waiting for transfers between devices, local(): block = lax.all_to_all(field, 'gy', split_axis=3, concat_axis=4, tiled=True)  10.8 us
    all_to_all x2, local copies, waits for them, and re-layouts, local(): return lax.all_to_all(final, 'gy', split_axis=4, concat_axis=3, tiled=True)  9.34 us
    another operation x4, local copies, waits for them, and re-layouts, complex_apply(): return jnp.stack([out_re, out_im], axis=1)  9.2 us
    all_to_all x1, starting transfers between devices, local(): block = lax.all_to_all(field, 'gy', split_axis=3, concat_axis=4, tiled=True)  6.03 us
  transfers between devices with their start and end apart: 5, of which 5 were waited for; matrix products, arithmetic and copies ran while one was open for 0% of the time, Pallas kernels for 0%

commit v1 on v0

v1 whole, which is shorter than its diff:
```python
import math

import jax
import jax.numpy as jnp
import numpy as np
from jax import lax
from jax.experimental import pallas as pl
from jax.experimental.pallas import tpu as pltpu
from jax.sharding import PartitionSpec as P

N = 2048
KZ_FIRST = 128
K0 = 512
GX = 16
GY = 8
ROWS = N // GX
COLS = N // GY
LANES = 128
PLANE = ("gx", "gy")


def reversed_bits(value, nbits):
    return sum(((value >> place) & 1) << (nbits - 1 - place) for place in range(nbits))


def outer_table():
    y0 = np.arange(16)[:, None, None, None, None]
    residue = np.array([reversed_bits(d, 4) for d in range(16)])[None, :, None, None, None]
    half = np.arange(2)[None, None, :, None, None]
    high = np.arange(16)[None, None, None, :, None]
    block = np.arange(8)[None, None, None, None, :]
    phase = (high * residue + (2 * block + half) * y0) % 16
    angle = (2.0 * math.pi / 16) * phase.reshape(256, 256)
    cos, sin = np.cos(angle), np.sin(angle)
    return np.block([[cos, -sin], [sin, cos]]).astype(np.float32)


def lane_table():
    lane = np.arange(LANES)
    y1 = 16 * (lane & 7) + 8 * ((lane >> 3) & 1) + (lane >> 4)
    angle = (2.0 * math.pi / LANES) * (lane[:, None] * y1[None, :] % LANES)
    cos, sin = np.cos(angle), np.sin(angle)
    return np.block([[cos, sin], [-sin, cos]]).astype(np.float32)


def twist_table():
    angle = (2.0 * math.pi / N) * (np.arange(16)[:, None] * np.arange(LANES)[None, :] % N)
    return np.stack([np.cos(angle), np.sin(angle)]).astype(np.float32)


def row_table():
    index = np.arange(ROWS)
    angle = (2.0 * math.pi / ROWS) * (index[:, None] * index[None, :] % ROWS)
    cos, sin = np.cos(angle), np.sin(angle)
    return np.block([[cos, -sin], [sin, cos]]).astype(np.float32)


def halves(value):
    high = value.astype(jnp.bfloat16)
    return high, (value - high.astype(jnp.float32)).astype(jnp.bfloat16)


def mac(left_high, left_low, right_high, right_low):
    def dot(left, right):
        return jnp.dot(left, right, preferred_element_type=jnp.float32)

    return dot(left_high, right_high) + (dot(left_high, right_low) + dot(left_low, right_high))


def pack_kernel(tor_ref, pol_ref, out_ref):
    for part in range(4):
        source = tor_ref if part < 2 else pol_ref
        for half in range(2):
            out_ref[pl.ds(part * 2 + half, ROWS, stride=8), :] = source[
                part % 2, 0, :, half * LANES : (half + 1) * LANES
            ]


def plane_kernel(in_ref, outer_ref, lane_ref, twist_ref, out_ref, high_ref, low_ref):
    low_x = lax.axis_index("gx") * GY + lax.axis_index("gy")
    wave_z = (KZ_FIRST + lax.axis_index("gz")).astype(jnp.float32)
    row = lax.broadcasted_iota(jnp.int32, (ROWS, LANES), 0)
    lane = lax.broadcasted_iota(jnp.int32, (ROWS, LANES), 1)
    glob_x = (row >> 3) * ROWS + low_x
    wave_x = jnp.where(glob_x < N // 2, glob_x, glob_x - N).astype(jnp.float32)
    for half in range(2):
        glob_y = (row & 7) * COLS + (half * LANES + lane)
        wave_y = jnp.where(glob_y < N // 2, glob_y, glob_y - N).astype(jnp.float32)
        horiz = wave_x * wave_x + wave_y * wave_y
        square = horiz + wave_z * wave_z
        pol_gain = (4.0 / N / (K0 * K0)) * jnp.exp(1.0 - square * (1.0 / (K0 * K0)))
        tor_gain = pol_gain * jnp.sqrt(square)
        parts = [in_ref[pl.ds(part * 2 + half, ROWS, stride=8), :] for part in range(4)]
        tor_re, tor_im = parts[0] * tor_gain, parts[1] * tor_gain
        pol_re, pol_im = parts[2] * pol_gain, parts[3] * pol_gain
        cross_x, cross_y = wave_x * wave_z, wave_y * wave_z
        spectrum = [
            (-wave_y * tor_im - cross_x * pol_re, wave_y * tor_re - cross_x * pol_im),
            (wave_x * tor_im - cross_y * pol_re, -wave_x * tor_re - cross_y * pol_im),
            (horiz * pol_re, horiz * pol_im),
        ]
        for comp in range(3):
            for imag in range(2):
                high, low = halves(spectrum[comp][imag])
                at = pl.ds(imag * 256 + half * ROWS, ROWS), pl.ds(comp * LANES, LANES)
                high_ref[at] = high
                low_ref[at] = low
    residue = reversed_bits(lax.broadcasted_iota(jnp.int32, (GX, LANES), 0), 4)
    angle = (low_x * residue % N).astype(jnp.float32) * (2.0 * math.pi / N)
    turn_re, turn_im = jnp.cos(angle)[None], jnp.sin(angle)[None]
    beta_re, beta_im = twist_ref[0][:, None, :], twist_ref[1][:, None, :]
    twist_re = (beta_re * turn_re - beta_im * turn_im).reshape(256, LANES)
    twist_im = (beta_re * turn_im + beta_im * turn_re).reshape(256, LANES)
    outer_high, outer_low = halves(outer_ref[...])
    lane_high, lane_low = halves(lane_ref[...])
    lane_bit = lax.broadcasted_iota(jnp.int32, (GX, LANES), 1)
    for comp in range(3):
        cols = slice(comp * LANES, (comp + 1) * LANES)
        value = mac(outer_high, outer_low, high_ref[:, cols], low_ref[:, cols])
        real, imag = value[:256], value[256:]
        turned = jnp.concatenate(
            [real * twist_re - imag * twist_im, real * twist_im + imag * twist_re], axis=1
        )
        high, low = halves(turned)
        value = mac(high, low, lane_high, lane_low)
        for imag in range(2):
            tiles = [
                value[y0 * GX : (y0 + 1) * GX, imag * LANES : (imag + 1) * LANES] for y0 in range(16)
            ]
            for place in range(4):
                step = 1 << place
                upper = (lane_bit & step) != 0
                swapped = list(tiles)
                for index in range(16):
                    if index & step:
                        continue
                    first, second = tiles[index], tiles[index | step]
                    swapped[index] = jnp.where(upper, pltpu.roll(second, step, 1), first)
                    swapped[index | step] = jnp.where(
                        upper, second, pltpu.roll(first, LANES - step, 1)
                    )
                tiles = swapped
            for index in range(16):
                start = (index & 7) * 12 + (comp * 2 + imag) * 2 + (index >> 3)
                out_ref[pl.ds(start, GX, stride=96), :] = tiles[index]


def row_kernel(in_ref, table_ref, out_ref):
    table_high, table_low = halves(table_ref[...])
    for comp in range(3):
        parts = [
            jnp.concatenate(
                [in_ref[pl.ds((comp * 2 + imag) * 2 + half, ROWS, stride=12), :] for half in range(2)],
                axis=1,
            )
            for imag in range(2)
        ]
        high, low = halves(jnp.concatenate(parts, axis=0))
        value = mac(table_high, table_low, high, low)
        out_ref[comp, 0, 0] = value[:ROWS]
        out_ref[comp, 1, 0] = value[ROWS:]


def exchange(value):
    chunks = value.reshape(GX * GY, 1, -1)
    return lax.all_to_all(chunks, PLANE, 0, 0, tiled=True).reshape(-1, LANES)


def local(toroidal, poloidal):
    vmem = pl.BlockSpec(memory_space=pltpu.VMEM)
    packed = pl.pallas_call(
        pack_kernel,
        out_shape=jax.ShapeDtypeStruct((ROWS * 8, LANES), jnp.float32),
        in_specs=[vmem, vmem],
        out_specs=vmem,
    )(toroidal, poloidal)
    spread = exchange(packed)
    lines = pl.pallas_call(
        plane_kernel,
        out_shape=jax.ShapeDtypeStruct((ROWS * 12, LANES), jnp.float32),
        in_specs=[vmem] * 4,
        out_specs=vmem,
        scratch_shapes=[pltpu.VMEM((512, 3 * LANES), jnp.bfloat16)] * 2,
        compiler_params=pltpu.CompilerParams(vmem_limit_bytes=32 * 2**20),
    )(spread, outer_table(), lane_table(), twist_table())
    gathered = exchange(lines)
    return pl.pallas_call(
        row_kernel,
        out_shape=jax.ShapeDtypeStruct((3, 2, 1, ROWS, COLS), jnp.float32),
        in_specs=[vmem, vmem],
        out_specs=vmem,
        compiler_params=pltpu.CompilerParams(vmem_limit_bytes=32 * 2**20),
    )(gathered, row_table())


def solution(mesh):
    in_specs = (P(None, "gz", "gx", "gy"), P(None, "gz", "gx", "gy"))
    out_specs = P(None, None, "gz", "gx", "gy")
    return jax.shard_map(local, mesh=mesh, in_specs=in_specs, out_specs=out_specs, check_vma=False)
```

time: 210 us -> 73.2 us (0.35)
  waiting for transfers between devices: 112 us -> 0 us
  blocking collectives: 14.6 us -> 65.6 us
  local copies, waits for them, and re-layouts: 45.6 us -> 0.02 us
  starting transfers between devices: 17 us -> 0 us
  matrix products: 13.2 us -> 0 us
  Pallas kernels: 0 us -> 7.35 us
  other arithmetic: 6.38 us -> 0 us
    ppermute x4 -> x0, waiting for transfers between devices: 102 us -> none  [swapped(): return lax.ppermute(value, axis, pairs)]
    all_to_all x1 -> x2, blocking collectives: 14.6 us -> 65.6 us  [exchange(): return lax.all_to_all(chunks, PLANE, 0, 0, tiled=True).reshape(-1, LANES)]
    unnamed x10 -> x8, local copies, waits for them, and re-layouts: 22.2 us -> 0.02 us
    dot_general x12 -> x0, matrix products: 13.2 us -> none  [the longest x3 3.74 us: complex_apply(): jnp.einsum(form, table_im, real_part, precision=high)]
    ppermute x4 -> x0, starting transfers between devices: 11 us -> none  [swapped(): return lax.ppermute(value, axis, pairs)]
    all_to_all x1 -> x0, waiting for transfers between devices: 10.8 us -> none  [local(): block = lax.all_to_all(field, 'gy', split_axis=3, concat_axis=4, tiled=True)]
    all_to_all x4 -> x0, local copies, waits for them, and re-layouts: 9.86 us -> none  [the longest x2 9.34 us: local(): return lax.all_to_all(final, 'gy', split_axis=4, concat_axis=3, tiled=True)]
    another operation x4 -> x0, local copies, waits for them, and re-layouts: 9.2 us -> none  [complex_apply(): return jnp.stack([out_re, out_im], axis=1)]
  transfers between devices with their start and end apart: 5 -> 0, of which waited for: 5 -> 0; matrix products, arithmetic and copies ran while one was open for 0% -> 0% of each run, Pallas kernels for 0% -> 0%
where the time goes in v1:
time: 73.2 us; the launch traced here: 72.9 us
  blocking collectives  65.6 us (90%)
  Pallas kernels  7.35 us (10%)
    all_to_all x2, blocking collectives, exchange(): return lax.all_to_all(chunks, PLANE, 0, 0, tiled=True).reshape(-1, LANES)  65.6 us
    pallas_call x1, Pallas kernels, local(): pl.pallas_call(plane_kernel, out_shape=jax.ShapeDtypeStruct((ROWS * 12, L...  3.94 us
    pallas_call x1, Pallas kernels, local(): pl.pallas_call(pack_kernel, out_shape=jax.ShapeDtypeStruct((ROWS * 8, LAN...  2.04 us

profile of v1, /device:TPU:8, one launch (start us, length us, event | category | flops | bytes accessed | tf_op | source)
XLA Modules:
  0.0 72.9 jit_solution(16708936088069419710)
XLA Ops:
  0.0 0.0 copy-start
  0.0 2.0 %shard_map.64 = f32[1024,128]{1,0:T(8,128)} custom-call(f32[2,1,128,256]{3,2,1,0:T(8,128)} %tor_ref.1, f32[2,1,128,256]{3,2,1,0:T(8,128)} %pol_ref.1), custom_call_target="tpu_custom_call" | custom-call | tf_op jit(solution)/shard_map/pallas_call | solution.py:171
  2.0 0.0 copy-start.2
  2.0 0.0 copy-start.3
  2.1 35.0 %all_to_all.10 = f32[128,1,1024]{2,1,0:T(1,128)S(1)} all-to-all(f32[128,1,1024]{2,1,0:T(1,128)} %bitcast.7), channel_id=1, replica_groups=mesh['gx'=16,'gy'=8,'gz'=2] {'gx','gy'}, dimensions={0} | all-to-all | bytes 1048576 | tf_op jit(solution)/shard_map/all_to_all | solution.py:166
  37.0 0.0 copy-done
  37.0 0.0 copy-done.2
  37.0 0.0 copy-done.3
  37.0 3.9 %shard_map.65 = f32[1536,128]{1,0:T(8,128)S(1)} custom-call(f32[1024,128]{1,0:T(8,128)S(1)} %bitcast.6, f32[512,512]{1,0:T(8,128)S(1)} %copy-done, f32[256,256]{1,0:T(8,128)S(1)} %copy-done.2, f32[2,16,128]{2,1,0:T(8,128)S(1)} %copy-done.3), custom_call_target="tpu_custom_call" | custom-call | tf_op jit(solution)/shard_map/pallas_call | solution.py:178
  41.0 0.0 copy-start.1
  41.0 30.6 %all_to_all.11 = f32[128,1,1536]{2,1,0:T(1,128)S(1)} all-to-all(f32[128,1,1536]{2,1,0:T(1,128)S(1)} %bitcast.5), channel_id=1, replica_groups=mesh['gx'=16,'gy'=8,'gz'=2] {'gx','gy'}, dimensions={0} | all-to-all | bytes 1572864 | tf_op jit(solution)/shard_map/all_to_all | solution.py:166
  71.6 0.0 copy-done.1
  71.6 1.4 %shard_map.66 = f32[3,2,1,128,256]{4,3,2,1,0:T(8,128)} custom-call(f32[1536,128]{1,0:T(8,128)S(1)} %bitcast.4, f32[256,256]{1,0:T(8,128)S(1)} %copy-done.1), custom_call_target="tpu_custom_call" | custom-call | tf_op jit(solution)/shard_map/pallas_call | solution.py:187
Async XLA Ops:
  0.0 37.0 %copy-start = (f32[512,512]{1,0:T(8,128)S(1)}, f32[512,512]{1,0:T(8,128)}, u32[]{:S(2)}) copy-start(f32[512,512]{1,0:T(8,128)} %constant.8.clone.outer_ref) | copy-start | bytes 3145732
  2.0 35.0 %copy-start.2 = (f32[256,256]{1,0:T(8,128)S(1)}, f32[256,256]{1,0:T(8,128)}, u32[]{:S(2)}) copy-start(f32[256,256]{1,0:T(8,128)} %constant.9.clone.lane_ref) | copy-start | bytes 786436
  2.0 35.0 %copy-start.3 = (f32[2,16,128]{2,1,0:T(8,128)S(1)}, f32[2,16,128]{2,1,0:T(8,128)}, u32[]{:S(2)}) copy-start(f32[2,16,128]{2,1,0:T(8,128)} %constant.10.clone.twist_ref) | copy-start | bytes 49156
  41.0 30.6 %copy-start.1 = (f32[256,256]{1,0:T(8,128)S(1)}, f32[256,256]{1,0:T(8,128)}, u32[]{:S(2)}) copy-start(f32[256,256]{1,0:T(8,128)} %constant.11.clone.table_ref) | copy-start | bytes 786436

commit v2 on v1

--- a/solution.py
+++ b/solution.py
@@ -2,6 +2,7 @@
 
 import jax
 import jax.numpy as jnp
+import ml_dtypes
 import numpy as np
 from jax import lax
 from jax.experimental import pallas as pl
@@ -23,16 +24,24 @@
     return sum(((value >> place) & 1) << (nbits - 1 - place) for place in range(nbits))
 
 
-def outer_table():
-    y0 = np.arange(16)[:, None, None, None, None]
-    residue = np.array([reversed_bits(d, 4) for d in range(16)])[None, :, None, None, None]
-    half = np.arange(2)[None, None, :, None, None]
-    high = np.arange(16)[None, None, None, :, None]
-    block = np.arange(8)[None, None, None, None, :]
-    phase = (high * residue + (2 * block + half) * y0) % 16
-    angle = (2.0 * math.pi / 16) * phase.reshape(256, 256)
-    cos, sin = np.cos(angle), np.sin(angle)
-    return np.block([[cos, -sin], [sin, cos]]).astype(np.float32)
+def split_table(values, axis):
+    high = values.astype(ml_dtypes.bfloat16)
+    low = (values - high.astype(np.float64)).astype(ml_dtypes.bfloat16)
+    return np.concatenate([high, low], axis)
+
+
+def outer_tables():
+    y0 = np.arange(8)[:, None, None, None]
+    residue = np.array([reversed_bits(d, 4) for d in range(GX)])[None, :, None, None]
+    high = np.arange(GX)[None, None, :, None]
+    block = np.arange(GY)[None, None, None, :]
+    tables = []
+    for half in range(2):
+        phase = (high * residue + (2 * block + half) * y0) % 16
+        angle = (2.0 * math.pi / 16) * phase.reshape(128, 128)
+        cos, sin = np.cos(angle), np.sin(angle)
+        tables.append(split_table(np.block([[cos, -sin], [sin, cos]]), 1))
+    return np.stack(tables)
 
 
 def lane_table():
@@ -40,7 +49,7 @@
     y1 = 16 * (lane & 7) + 8 * ((lane >> 3) & 1) + (lane >> 4)
     angle = (2.0 * math.pi / LANES) * (lane[:, None] * y1[None, :] % LANES)
     cos, sin = np.cos(angle), np.sin(angle)
-    return np.block([[cos, sin], [-sin, cos]]).astype(np.float32)
+    return split_table(np.block([[cos, sin], [-sin, cos]]), 0)
 
 
 def twist_table():
@@ -52,7 +61,7 @@
     index = np.arange(ROWS)
     angle = (2.0 * math.pi / ROWS) * (index[:, None] * index[None, :] % ROWS)
     cos, sin = np.cos(angle), np.sin(angle)
-    return np.block([[cos, -sin], [sin, cos]]).astype(np.float32)
+    return split_table(np.block([[cos, -sin], [sin, cos]]), 1)
 
 
 def halves(value):
@@ -60,11 +69,13 @@
     return high, (value - high.astype(jnp.float32)).astype(jnp.bfloat16)
 
 
-def mac(left_high, left_low, right_high, right_low):
-    def dot(left, right):
-        return jnp.dot(left, right, preferred_element_type=jnp.float32)
-
-    return dot(left_high, right_high) + (dot(left_high, right_low) + dot(left_low, right_high))
+def dot(left, right):
+    return jnp.dot(left, right, preferred_element_type=jnp.float32)
+
+
+def table_times(table, high, low):
+    wide = jnp.concatenate([table, table[:, : table.shape[1] // 2]], axis=1)
+    return dot(wide, jnp.concatenate([high, high, low], axis=0))
 
 
 def pack_kernel(tor_ref, pol_ref, out_ref):
@@ -102,7 +113,7 @@
         for comp in range(3):
             for imag in range(2):
                 high, low = halves(spectrum[comp][imag])
-                at = pl.ds(imag * 256 + half * ROWS, ROWS), pl.ds(comp * LANES, LANES)
+                at = half, pl.ds(imag * ROWS, ROWS), pl.ds(comp * LANES, LANES)
                 high_ref[at] = high
                 low_ref[at] = low
     residue = reversed_bits(lax.broadcasted_iota(jnp.int32, (GX, LANES), 0), 4)
@@ -111,18 +122,20 @@
     beta_re, beta_im = twist_ref[0][:, None, :], twist_ref[1][:, None, :]
     twist_re = (beta_re * turn_re - beta_im * turn_im).reshape(256, LANES)
     twist_im = (beta_re * turn_im + beta_im * turn_re).reshape(256, LANES)
-    outer_high, outer_low = halves(outer_ref[...])
-    lane_high, lane_low = halves(lane_ref[...])
+    table = lane_ref[...]
+    lane_wide = jnp.concatenate([table[:256], table[:256], table[256:]], axis=0)
     lane_bit = lax.broadcasted_iota(jnp.int32, (GX, LANES), 1)
+    even, odd = [table_times(outer_ref[h], high_ref[h], low_ref[h]) for h in range(2)]
     for comp in range(3):
         cols = slice(comp * LANES, (comp + 1) * LANES)
-        value = mac(outer_high, outer_low, high_ref[:, cols], low_ref[:, cols])
-        real, imag = value[:256], value[256:]
+        total, differ = even[:, cols] + odd[:, cols], even[:, cols] - odd[:, cols]
+        real = jnp.concatenate([total[:ROWS], differ[:ROWS]], axis=0)
+        imag = jnp.concatenate([total[ROWS:], differ[ROWS:]], axis=0)
         turned = jnp.concatenate(
             [real * twist_re - imag * twist_im, real * twist_im + imag * twist_re], axis=1
         )
         high, low = halves(turned)
-        value = mac(high, low, lane_high, lane_low)
+        value = dot(jnp.concatenate([high, low, high], axis=1), lane_wide)
         for imag in range(2):
             tiles = [
                 value[y0 * GX : (y0 + 1) * GX, imag * LANES : (imag + 1) * LANES] for y0 in range(16)
@@ -146,7 +159,6 @@
 
 
 def row_kernel(in_ref, table_ref, out_ref):
-    table_high, table_low = halves(table_ref[...])
     for comp in range(3):
         parts = [
             jnp.concatenate(
@@ -156,7 +168,7 @@
             for imag in range(2)
         ]
         high, low = halves(jnp.concatenate(parts, axis=0))
-        value = mac(table_high, table_low, high, low)
+        value = table_times(table_ref[...], high, low)
         out_ref[comp, 0, 0] = value[:ROWS]
         out_ref[comp, 1, 0] = value[ROWS:]
 
@@ -180,9 +192,9 @@
         out_shape=jax.ShapeDtypeStruct((ROWS * 12, LANES), jnp.float32),
         in_specs=[vmem] * 4,
         out_specs=vmem,
-        scratch_shapes=[pltpu.VMEM((512, 3 * LANES), jnp.bfloat16)] * 2,
+        scratch_shapes=[pltpu.VMEM((2, 256, 3 * LANES), jnp.bfloat16)] * 2,
         compiler_params=pltpu.CompilerParams(vmem_limit_bytes=32 * 2**20),
-    )(spread, outer_table(), lane_table(), twist_table())
+    )(spread, outer_tables(), lane_table(), twist_table())
     gathered = exchange(lines)
     return pl.pallas_call(
         row_kernel,

time: 73.2 us -> 71.3 us (0.974)
  Pallas kernels: 7.35 us -> 5.5 us
    pallas_call x1, Pallas kernels: 3.94 us -> 2.17 us  [local(): pl.pallas_call(plane_kernel, out_shape=jax.ShapeDtypeStruct((ROWS * 12, L...]
where the time goes in v2:
time: 71.3 us; the launch traced here: 71.1 us
  blocking collectives  65.6 us (92%)
  Pallas kernels  5.5 us (8%)
    all_to_all x2, blocking collectives, exchange(): return lax.all_to_all(chunks, PLANE, 0, 0, tiled=True).reshape(-1, LANES)  65.6 us
    pallas_call x1, Pallas kernels, local(): pl.pallas_call(plane_kernel, out_shape=jax.ShapeDtypeStruct((ROWS * 12, L...  2.17 us
    pallas_call x1, Pallas kernels, local(): pl.pallas_call(pack_kernel, out_shape=jax.ShapeDtypeStruct((ROWS * 8, LAN...  1.95 us

profile of v2, /device:TPU:8, one launch (start us, length us, event | category | flops | bytes accessed | tf_op | source)
XLA Modules:
  0.0 71.1 jit_solution(3362352048633170765)
XLA Ops:
  0.0 2.0 %shard_map.64 = f32[1024,128]{1,0:T(8,128)} custom-call(f32[2,1,128,256]{3,2,1,0:T(8,128)} %tor_ref.1, f32[2,1,128,256]{3,2,1,0:T(8,128)} %pol_ref.1), custom_call_target="tpu_custom_call" | custom-call | tf_op jit(solution)/shard_map/pallas_call | solution.py:183
  2.0 0.0 copy-start
  2.0 0.0 copy-start.2
  2.0 0.0 copy-start.3
  2.0 35.0 %all_to_all.10 = f32[128,1,1024]{2,1,0:T(1,128)S(1)} all-to-all(f32[128,1,1024]{2,1,0:T(1,128)} %bitcast.7), channel_id=1, replica_groups=mesh['gx'=16,'gy'=8,'gz'=2] {'gx','gy'}, dimensions={0} | all-to-all | bytes 1048576 | tf_op jit(solution)/shard_map/all_to_all | solution.py:178
  36.9 0.0 copy-done
  36.9 0.0 copy-done.2
  36.9 0.0 copy-done.3
  36.9 2.2 %shard_map.65 = f32[1536,128]{1,0:T(8,128)S(1)} custom-call(f32[1024,128]{1,0:T(8,128)S(1)} %bitcast.6, bf16[2,256,512]{2,1,0:T(8,128)(2,1)S(1)} %copy-done, bf16[512,256]{1,0:T(8,128)(2,1)S(1)} %copy-done.2, f32[2,16,128]{2,1,0:T(8,128)S(1)} %copy-done.3), custom_call_target="tpu_custom_call" | custom-call | tf_op jit(solution)/shard_map/pallas_call | solution.py:190
  39.1 0.0 copy-start.1
  39.1 30.6 %all_to_all.11 = f32[128,1,1536]{2,1,0:T(1,128)S(1)} all-to-all(f32[128,1,1536]{2,1,0:T(1,128)S(1)} %bitcast.5), channel_id=1, replica_groups=mesh['gx'=16,'gy'=8,'gz'=2] {'gx','gy'}, dimensions={0} | all-to-all | bytes 1572864 | tf_op jit(solution)/shard_map/all_to_all | solution.py:178
  69.7 0.0 copy-done.1
  69.7 1.4 %shard_map.66 = f32[3,2,1,128,256]{4,3,2,1,0:T(8,128)} custom-call(f32[1536,128]{1,0:T(8,128)S(1)} %bitcast.4, bf16[256,512]{1,0:T(8,128)(2,1)S(1)} %copy-done.1), custom_call_target="tpu_custom_call" | custom-call | tf_op jit(solution)/shard_map/pallas_call | solution.py:199
Async XLA Ops:
  2.0 35.0 %copy-start = (bf16[2,256,512]{2,1,0:T(8,128)(2,1)S(1)}, bf16[2,256,512]{2,1,0:T(8,128)(2,1)}, u32[]{:S(2)}) copy-start(bf16[2,256,512]{2,1,0:T(8,128)(2,1)} %constant.8.clone.outer_ref) | copy-start | bytes 1572868
  2.0 35.0 %copy-start.2 = (bf16[512,256]{1,0:T(8,128)(2,1)S(1)}, bf16[512,256]{1,0:T(8,128)(2,1)}, u32[]{:S(2)}) copy-start(bf16[512,256]{1,0:T(8,128)(2,1)} %constant.9.clone.lane_ref) | copy-start | bytes 786436
  2.0 35.0 %copy-start.3 = (f32[2,16,128]{2,1,0:T(8,128)S(1)}, f32[2,16,128]{2,1,0:T(8,128)}, u32[]{:S(2)}) copy-start(f32[2,16,128]{2,1,0:T(8,128)} %constant.10.clone.twist_ref) | copy-start | bytes 49156
  39.1 30.6 %copy-start.1 = (bf16[256,512]{1,0:T(8,128)(2,1)S(1)}, bf16[256,512]{1,0:T(8,128)(2,1)}, u32[]{:S(2)}) copy-start(bf16[256,512]{1,0:T(8,128)(2,1)} %constant.11.clone.table_ref) | copy-start | bytes 786436

commit v3 on v2

--- a/solution.py
+++ b/solution.py
@@ -17,7 +17,10 @@
 ROWS = N // GX
 COLS = N // GY
 LANES = 128
-PLANE = ("gx", "gy")
+PLANE = ("gx", "gy", "gz")
+GX_ORDER = [11, 7, 15, 6, 13, 5, 9, 4, 10, 3, 12, 2, 8, 1, 14, 0]
+GY_ORDER = [7, 5, 3, 6, 1, 4, 2, 0]
+ORDER = [gx * GY + gy for gx in GX_ORDER for gy in GY_ORDER]
 
 
 def reversed_bits(value, nbits):
@@ -31,10 +34,10 @@
 
 
 def outer_tables():
-    y0 = np.arange(8)[:, None, None, None]
-    residue = np.array([reversed_bits(d, 4) for d in range(GX)])[None, :, None, None]
-    high = np.arange(GX)[None, None, :, None]
-    block = np.arange(GY)[None, None, None, :]
+    y0 = np.arange(8)[:, None, None]
+    residue = np.array([reversed_bits(d, 4) for d in GX_ORDER])[None, :, None]
+    high = (np.array(ORDER) // GY)[None, None, :]
+    block = (np.array(ORDER) % GY)[None, None, :]
     tables = []
     for half in range(2):
         phase = (high * residue + (2 * block + half) * y0) % 16
@@ -46,7 +49,7 @@
 
 def lane_table():
     lane = np.arange(LANES)
-    y1 = 16 * (lane & 7) + 8 * ((lane >> 3) & 1) + (lane >> 4)
+    y1 = 16 * np.array(GY_ORDER)[lane & 7] + 8 * ((lane >> 3) & 1) + (lane >> 4)
     angle = (2.0 * math.pi / LANES) * (lane[:, None] * y1[None, :] % LANES)
     cos, sin = np.cos(angle), np.sin(angle)
     return split_table(np.block([[cos, sin], [-sin, cos]]), 0)
@@ -62,6 +65,19 @@
     angle = (2.0 * math.pi / ROWS) * (index[:, None] * index[None, :] % ROWS)
     cos, sin = np.cos(angle), np.sin(angle)
     return split_table(np.block([[cos, -sin], [sin, cos]]), 1)
+
+
+def turn_table():
+    residue = np.array([reversed_bits(d, 4) for d in GX_ORDER], np.float32) / N
+    return np.broadcast_to(residue[:, None], (GX, LANES)).copy()
+
+
+def wave_table():
+    sender = np.array(ORDER)
+    base_x = (sender // GY + GX // 2) % GX * ROWS - N // 2
+    base_y = (sender % GY + GY // 2) % GY * COLS - N // 2
+    rows = np.stack([base_x, base_y]).astype(np.float32)
+    return np.broadcast_to(rows[:, :, None], (2, ROWS, LANES)).copy()
 
 
 def halves(value):
@@ -87,16 +103,19 @@
             ]
 
 
-def plane_kernel(in_ref, outer_ref, lane_ref, twist_ref, out_ref, high_ref, low_ref):
-    low_x = lax.axis_index("gx") * GY + lax.axis_index("gy")
+def place_in(order, device):
+    return sum(jnp.where(device == entry, place, 0) for place, entry in enumerate(order))
+
+
+def plane_kernel(
+    in_ref, outer_ref, lane_ref, twist_ref, turn_ref, wave_ref, out_ref, high_ref, low_ref
+):
+    low_x = place_in(GX_ORDER, lax.axis_index("gx")) * GY + place_in(GY_ORDER, lax.axis_index("gy"))
     wave_z = (KZ_FIRST + lax.axis_index("gz")).astype(jnp.float32)
-    row = lax.broadcasted_iota(jnp.int32, (ROWS, LANES), 0)
-    lane = lax.broadcasted_iota(jnp.int32, (ROWS, LANES), 1)
-    glob_x = (row >> 3) * ROWS + low_x
-    wave_x = jnp.where(glob_x < N // 2, glob_x, glob_x - N).astype(jnp.float32)
+    lane = lax.broadcasted_iota(jnp.int32, (ROWS, LANES), 1).astype(jnp.float32)
+    wave_x = wave_ref[0] + low_x.astype(jnp.float32)
     for half in range(2):
-        glob_y = (row & 7) * COLS + (half * LANES + lane)
-        wave_y = jnp.where(glob_y < N // 2, glob_y, glob_y - N).astype(jnp.float32)
+        wave_y = wave_ref[1] + (lane + half * LANES)
         horiz = wave_x * wave_x + wave_y * wave_y
         square = horiz + wave_z * wave_z
         pol_gain = (4.0 / N / (K0 * K0)) * jnp.exp(1.0 - square * (1.0 / (K0 * K0)))
@@ -116,8 +135,8 @@
                 at = half, pl.ds(imag * ROWS, ROWS), pl.ds(comp * LANES, LANES)
                 high_ref[at] = high
                 low_ref[at] = low
-    residue = reversed_bits(lax.broadcasted_iota(jnp.int32, (GX, LANES), 0), 4)
-    angle = (low_x * residue % N).astype(jnp.float32) * (2.0 * math.pi / N)
+    turns = low_x.astype(jnp.float32) * turn_ref[...]
+    angle = (turns - jnp.floor(turns)) * (2.0 * math.pi)
     turn_re, turn_im = jnp.cos(angle)[None], jnp.sin(angle)[None]
     beta_re, beta_im = twist_ref[0][:, None, :], twist_ref[1][:, None, :]
     twist_re = (beta_re * turn_re - beta_im * turn_im).reshape(256, LANES)
@@ -175,7 +194,9 @@
 
 def exchange(value):
     chunks = value.reshape(GX * GY, 1, -1)
-    return lax.all_to_all(chunks, PLANE, 0, 0, tiled=True).reshape(-1, LANES)
+    groups = [[device * 2 + plane for device in ORDER] for plane in range(2)]
+    moved = lax.all_to_all(chunks, PLANE, 0, 0, axis_index_groups=groups, tiled=True)
+    return moved.reshape(-1, LANES)
 
 
 def local(toroidal, poloidal):
@@ -190,11 +211,11 @@
     lines = pl.pallas_call(
         plane_kernel,
         out_shape=jax.ShapeDtypeStruct((ROWS * 12, LANES), jnp.float32),
-        in_specs=[vmem] * 4,
+        in_specs=[vmem] * 6,
         out_specs=vmem,
         scratch_shapes=[pltpu.VMEM((2, 256, 3 * LANES), jnp.bfloat16)] * 2,
         compiler_params=pltpu.CompilerParams(vmem_limit_bytes=32 * 2**20),
-    )(spread, outer_tables(), lane_table(), twist_table())
+    )(spread, outer_tables(), lane_table(), twist_table(), turn_table(), wave_table())
     gathered = exchange(lines)
     return pl.pallas_call(
         row_kernel,

time: 71.3 us -> 66.5 us (0.933)
  blocking collectives: 65.6 us -> 60.1 us
    all_to_all x2, blocking collectives: 65.6 us -> 60.1 us  [exchange(): lax.all_to_all(chunks, PLANE, 0, 0, axis_index_groups=groups, tiled=True)]
where the time goes in v3:
time: 66.5 us; the launch traced here: 65.7 us
  blocking collectives  60.1 us (90%)
  Pallas kernels  5.5 us (8%)
    all_to_all x2, blocking collectives, exchange(): lax.all_to_all(chunks, PLANE, 0, 0, axis_index_groups=groups, tiled=True)  60.1 us
    pallas_call x1, Pallas kernels, local(): pl.pallas_call(plane_kernel, out_shape=jax.ShapeDtypeStruct((ROWS * 12, L...  2.17 us
    pallas_call x1, Pallas kernels, local(): pl.pallas_call(pack_kernel, out_shape=jax.ShapeDtypeStruct((ROWS * 8, LAN...  1.95 us
    pallas_call x1, Pallas kernels, local(): pl.pallas_call(row_kernel, out_shape=jax.ShapeDtypeStruct((3, 2, 1, ROWS,...  1.37 us

profile of v3, /device:TPU:8, one launch (start us, length us, event | category | flops | bytes accessed | tf_op | source)
XLA Modules:
  0.0 65.7 jit_solution(15774219161155392035)
XLA Ops:
  0.0 2.0 %shard_map.82 = f32[1024,128]{1,0:T(8,128)} custom-call(f32[2,1,128,256]{3,2,1,0:T(8,128)} %tor_ref.1, f32[2,1,128,256]{3,2,1,0:T(8,128)} %pol_ref.1), custom_call_target="tpu_custom_call" | custom-call | tf_op jit(solution)/shard_map/pallas_call | solution.py:204
  2.0 0.0 copy-start
  2.0 0.0 copy-start.2
  2.0 0.0 copy-start.3
  2.0 0.0 copy-start.4
  2.0 0.0 copy-start.5
  2.0 29.5 %all_to_all.10 = f32[128,1,1024]{2,1,0:T(1,128)S(1)} all-to-all(f32[128,1,1024]{2,1,0:T(1,128)} %bitcast.7), channel_id=1, replica_groups={{190,186,182,188,178,184,180,176,126,122,118,124,114,120,116,112,254,25..., dimensions={0} | all-to-all | bytes 1048576 | tf_op jit(solution)/shard_map/all_to_all | solution.py:198
  31.5 0.0 copy-done
  31.5 0.0 copy-done.2
  31.5 0.0 copy-done.3
  31.5 0.0 copy-done.4
  31.5 0.0 copy-done.5
  31.5 2.2 %shard_map.83 = f32[1536,128]{1,0:T(8,128)S(1)} custom-call(f32[1024,128]{1,0:T(8,128)S(1)} %bitcast.6, bf16[2,256,512]{2,1,0:T(8,128)(2,1)S(1)} %copy-done, bf16[512,256]{1,0:T(8,128)(2,1)S(1)} %copy-done.2, f32[2,16,128]{2,1,0:T(8,128)S(1)} %copy-done.4, f32[16,128]{1,0:T(8,128)S(1)} %copy-done.5, f32[2,128,128]{2,1,0:T(8,128)S(1)} %copy-done.3), custom_call_target="tpu_custom_call" | custom-call | tf_op jit(solution)/shard_map/pallas_call | solution.py:211
  33.7 0.0 copy-start.1
  33.7 30.6 %all_to_all.11 = f32[128,1,1536]{2,1,0:T(1,128)S(1)} all-to-all(f32[128,1,1536]{2,1,0:T(1,128)S(1)} %bitcast.5), channel_id=1, replica_groups={{190,186,182,188,178,184,180,176,126,122,118,124,114,120,116,112,254,25..., dimensions={0} | all-to-all | bytes 1572864 | tf_op jit(solution)/shard_map/all_to_all | solution.py:198
  64.3 0.0 copy-done.1
  64.3 1.4 %shard_map.84 = f32[3,2,1,128,256]{4,3,2,1,0:T(8,128)} custom-call(f32[1536,128]{1,0:T(8,128)S(1)} %bitcast.4, bf16[256,512]{1,0:T(8,128)(2,1)S(1)} %copy-done.1), custom_call_target="tpu_custom_call" | custom-call | tf_op jit(solution)/shard_map/pallas_call | solution.py:220
Async XLA Ops:
  2.0 29.5 %copy-start = (bf16[2,256,512]{2,1,0:T(8,128)(2,1)S(1)}, bf16[2,256,512]{2,1,0:T(8,128)(2,1)}, u32[]{:S(2)}) copy-start(bf16[2,256,512]{2,1,0:T(8,128)(2,1)} %constant.12.clone.outer_ref) | copy-start | bytes 1572868
  2.0 29.5 %copy-start.2 = (bf16[512,256]{1,0:T(8,128)(2,1)S(1)}, bf16[512,256]{1,0:T(8,128)(2,1)}, u32[]{:S(2)}) copy-start(bf16[512,256]{1,0:T(8,128)(2,1)} %constant.13.clone.lane_ref) | copy-start | bytes 786436
  2.0 29.5 %copy-start.3 = (f32[2,128,128]{2,1,0:T(8,128)S(1)}, f32[2,128,128]{2,1,0:T(8,128)}, u32[]{:S(2)}) copy-start(f32[2,128,128]{2,1,0:T(8,128)} %constant.16.clone.wave_ref) | copy-start | bytes 393220
  2.0 29.5 %copy-start.4 = (f32[2,16,128]{2,1,0:T(8,128)S(1)}, f32[2,16,128]{2,1,0:T(8,128)}, u32[]{:S(2)}) copy-start(f32[2,16,128]{2,1,0:T(8,128)} %constant.14.clone.twist_ref) | copy-start | bytes 49156
  2.0 29.6 %copy-start.5 = (f32[16,128]{1,0:T(8,128)S(1)}, f32[16,128]{1,0:T(8,128)}, u32[]{:S(2)}) copy-start(f32[16,128]{1,0:T(8,128)} %constant.15.clone.turn_ref) | copy-start | bytes 24580
  33.7 30.6 %copy-start.1 = (bf16[256,512]{1,0:T(8,128)(2,1)S(1)}, bf16[256,512]{1,0:T(8,128)(2,1)}, u32[]{:S(2)}) copy-start(bf16[256,512]{1,0:T(8,128)(2,1)} %constant.17.clone.table_ref) | copy-start | bytes 786436

commit v4 on v3

--- a/solution.py
+++ b/solution.py
@@ -49,14 +49,14 @@
 
 def lane_table():
     lane = np.arange(LANES)
-    y1 = 16 * np.array(GY_ORDER)[lane & 7] + 8 * ((lane >> 3) & 1) + (lane >> 4)
+    y1 = 8 * (lane & 15) + (lane >> 4)
     angle = (2.0 * math.pi / LANES) * (lane[:, None] * y1[None, :] % LANES)
     cos, sin = np.cos(angle), np.sin(angle)
     return split_table(np.block([[cos, sin], [-sin, cos]]), 0)
 
 
 def twist_table():
-    angle = (2.0 * math.pi / N) * (np.arange(16)[:, None] * np.arange(LANES)[None, :] % N)
+    angle = (2.0 * math.pi / N) * (-127 * np.arange(16)[:, None] * np.arange(LANES)[None, :] % N)
     return np.stack([np.cos(angle), np.sin(angle)]).astype(np.float32)
 
 
@@ -92,15 +92,6 @@
 def table_times(table, high, low):
     wide = jnp.concatenate([table, table[:, : table.shape[1] // 2]], axis=1)
     return dot(wide, jnp.concatenate([high, high, low], axis=0))
-
-
-def pack_kernel(tor_ref, pol_ref, out_ref):
-    for part in range(4):
-        source = tor_ref if part < 2 else pol_ref
-        for half in range(2):
-            out_ref[pl.ds(part * 2 + half, ROWS, stride=8), :] = source[
-                part % 2, 0, :, half * LANES : (half + 1) * LANES
-            ]
 
 
 def place_in(order, device):
@@ -162,19 +153,14 @@
             for place in range(4):
                 step = 1 << place
                 upper = (lane_bit & step) != 0
-                swapped = list(tiles)
-                for index in range(16):
-                    if index & step:
-                        continue
-                    first, second = tiles[index], tiles[index | step]
-                    swapped[index] = jnp.where(upper, pltpu.roll(second, step, 1), first)
-                    swapped[index | step] = jnp.where(
-                        upper, second, pltpu.roll(first, LANES - step, 1)
-                    )
-                tiles = swapped
+                tiles = [jnp.where(upper, tiles[(t + step) % 16], tiles[t]) for t in range(16)]
             for index in range(16):
-                start = (index & 7) * 12 + (comp * 2 + imag) * 2 + (index >> 3)
-                out_ref[pl.ds(start, GX, stride=96), :] = tiles[index]
+                tile = tiles[-index % 16]
+                if index:
+                    source = (lane_bit & 112) + ((lane_bit + index) & 15)
+                    tile = jnp.take_along_axis(tile, source, axis=1, mode="promise_in_bounds")
+                start = GY_ORDER.index(index >> 1) * 12 + (comp * 2 + imag) * 2 + (index & 1)
+                out_ref[pl.ds(start, GX, stride=96), :] = tile
 
 
 def row_kernel(in_ref, table_ref, out_ref):
@@ -201,12 +187,8 @@
 
 def local(toroidal, poloidal):
     vmem = pl.BlockSpec(memory_space=pltpu.VMEM)
-    packed = pl.pallas_call(
-        pack_kernel,
-        out_shape=jax.ShapeDtypeStruct((ROWS * 8, LANES), jnp.float32),
-        in_specs=[vmem, vmem],
-        out_specs=vmem,
-    )(toroidal, poloidal)
+    parts = jnp.concatenate([toroidal, poloidal], axis=0)
+    packed = parts.reshape(4, ROWS, 2, LANES).transpose(1, 0, 2, 3)
     spread = exchange(packed)
     lines = pl.pallas_call(
         plane_kernel,

time: 66.5 us -> 65.2 us (0.980)
  Pallas kernels: 5.5 us -> 3.15 us
  other arithmetic: 0 us -> 1.06 us
    pallas_call x1 -> x0, Pallas kernels: 1.95 us -> none  [local(): pl.pallas_call(pack_kernel, out_shape=jax.ShapeDtypeStruct((ROWS * 8, LAN...]
    concatenate x0 -> x1, other arithmetic: none -> 1.06 us  [local(): parts = jnp.concatenate([toroidal, poloidal], axis=0)]
where the time goes in v4:
time: 65.2 us; the launch traced here: 64.4 us
  blocking collectives  59.6 us (91%)
  Pallas kernels  3.15 us (5%)
  other arithmetic  1.06 us (2%)
    all_to_all x2, blocking collectives, exchange(): lax.all_to_all(chunks, PLANE, 0, 0, axis_index_groups=groups, tiled=True)  59.6 us
    pallas_call x1, Pallas kernels, local(): pl.pallas_call(plane_kernel, out_shape=jax.ShapeDtypeStruct((ROWS * 12, L...  1.78 us
    pallas_call x1, Pallas kernels, local(): pl.pallas_call(row_kernel, out_shape=jax.ShapeDtypeStruct((3, 2, 1, ROWS,...  1.37 us

profile of v4, /device:TPU:8, one launch (start us, length us, event | category | flops | bytes accessed | tf_op | source)
XLA Modules:
  0.0 64.4 jit_solution(10499280785546123805)
XLA Ops:
  0.0 1.1 %pad_maximum_fusion = f32[4,1,128,256]{3,2,1,0:T(8,128)S(1)} fusion(f32[2,1,128,256]{3,2,1,0:T(8,128)} %param.9, f32[2,1,128,256]{3,2,1,0:T(8,128)} %param.8), kind=kLoop, calls=%fused_computation | loop fusion | flops 131072 | bytes 1048576 | tf_op jit(solution)/shard_map/concatenate | solution.py:190
  1.1 0.3 reshape.15
  1.3 0.2 copy.10
  1.5 0.0 copy-start
  1.5 0.0 copy-start.2
  1.6 0.0 copy-start.3
  1.6 0.0 copy-start.4
  1.6 0.0 copy-start.5
  1.6 29.1 %all_to_all.10 = f32[128,1,1024]{2,1,0:T(1,128)S(1)} all-to-all(f32[128,1,1024]{2,1,0:T(1,128)S(1)} %bitcast.11), channel_id=1, replica_groups={{190,186,182,188,178,184,180,176,126,122,118,124,114,120,116,112,254,25..., dimensions={0} | all-to-all | bytes 1048576 | tf_op jit(solution)/shard_map/all_to_all | solution.py:184
  30.7 0.0 copy-done
  30.7 0.0 copy-done.2
  30.7 0.0 copy-done.3
  30.8 0.0 copy-done.4
  30.8 0.0 copy-done.5
  30.8 1.8 %shard_map.82 = f32[1536,128]{1,0:T(8,128)S(1)} custom-call(f32[1024,128]{1,0:T(8,128)S(1)} %bitcast.10, bf16[2,256,512]{2,1,0:T(8,128)(2,1)S(1)} %copy-done, bf16[512,256]{1,0:T(8,128)(2,1)S(1)} %copy-done.2, f32[2,16,128]{2,1,0:T(8,128)S(1)} %copy-done.4, f32[16,128]{1,0:T(8,128)S(1)} %copy-done.5, f32[2,128,128]{2,1,0:T(8,128)S(1)} %copy-done.3), custom_call_target="tpu_custom_call" | custom-call | tf_op jit(solution)/shard_map/pallas_call | solution.py:193
  32.6 0.0 copy-start.1
  32.6 30.5 %all_to_all.11 = f32[128,1,1536]{2,1,0:T(1,128)S(1)} all-to-all(f32[128,1,1536]{2,1,0:T(1,128)S(1)} %bitcast.9), channel_id=1, replica_groups={{190,186,182,188,178,184,180,176,126,122,118,124,114,120,116,112,254,25..., dimensions={0} | all-to-all | bytes 1572864 | tf_op jit(solution)/shard_map/all_to_all | solution.py:184
  63.1 0.0 copy-done.1
  63.1 1.4 %shard_map.83 = f32[3,2,1,128,256]{4,3,2,1,0:T(8,128)} custom-call(f32[1536,128]{1,0:T(8,128)S(1)} %bitcast.8, bf16[256,512]{1,0:T(8,128)(2,1)S(1)} %copy-done.1), custom_call_target="tpu_custom_call" | custom-call | tf_op jit(solution)/shard_map/pallas_call | solution.py:202
Async XLA Ops:
  1.5 29.2 %copy-start = (bf16[2,256,512]{2,1,0:T(8,128)(2,1)S(1)}, bf16[2,256,512]{2,1,0:T(8,128)(2,1)}, u32[]{:S(2)}) copy-start(bf16[2,256,512]{2,1,0:T(8,128)(2,1)} %constant.12.clone.outer_ref) | copy-start | bytes 1572868
  1.5 29.2 %copy-start.2 = (bf16[512,256]{1,0:T(8,128)(2,1)S(1)}, bf16[512,256]{1,0:T(8,128)(2,1)}, u32[]{:S(2)}) copy-start(bf16[512,256]{1,0:T(8,128)(2,1)} %constant.13.clone.lane_ref) | copy-start | bytes 786436
  1.6 29.2 %copy-start.3 = (f32[2,128,128]{2,1,0:T(8,128)S(1)}, f32[2,128,128]{2,1,0:T(8,128)}, u32[]{:S(2)}) copy-start(f32[2,128,128]{2,1,0:T(8,128)} %constant.16.clone.wave_ref) | copy-start | bytes 393220
  1.6 29.2 %copy-start.4 = (f32[2,16,128]{2,1,0:T(8,128)S(1)}, f32[2,16,128]{2,1,0:T(8,128)}, u32[]{:S(2)}) copy-start(f32[2,16,128]{2,1,0:T(8,128)} %constant.14.clone.twist_ref) | copy-start | bytes 49156
  1.6 29.2 %copy-start.5 = (f32[16,128]{1,0:T(8,128)S(1)}, f32[16,128]{1,0:T(8,128)}, u32[]{:S(2)}) copy-start(f32[16,128]{1,0:T(8,128)} %constant.15.clone.turn_ref) | copy-start | bytes 24580
  32.6 30.5 %copy-start.1 = (bf16[256,512]{1,0:T(8,128)(2,1)S(1)}, bf16[256,512]{1,0:T(8,128)(2,1)}, u32[]{:S(2)}) copy-start(bf16[256,512]{1,0:T(8,128)(2,1)} %constant.17.clone.table_ref) | copy-start | bytes 786436

commit v5 on v4

--- a/solution.py
+++ b/solution.py
@@ -163,7 +163,8 @@
                 out_ref[pl.ds(start, GX, stride=96), :] = tile
 
 
-def row_kernel(in_ref, table_ref, out_ref):
+def row_kernel(in_ref, table_ref, out_ref, value_ref, sems):
+    copies = []
     for comp in range(3):
         parts = [
             jnp.concatenate(
@@ -174,8 +175,12 @@
         ]
         high, low = halves(jnp.concatenate(parts, axis=0))
         value = table_times(table_ref[...], high, low)
-        out_ref[comp, 0, 0] = value[:ROWS]
-        out_ref[comp, 1, 0] = value[ROWS:]
+        value_ref[comp, 0] = value[:ROWS]
+        value_ref[comp, 1] = value[ROWS:]
+        copies.append(pltpu.make_async_copy(value_ref.at[comp], out_ref.at[comp, :, 0], sems.at[comp]))
+        copies[-1].start()
+    for copy in copies:
+        copy.wait()
 
 
 def exchange(value):
@@ -188,7 +193,8 @@
 def local(toroidal, poloidal):
     vmem = pl.BlockSpec(memory_space=pltpu.VMEM)
     parts = jnp.concatenate([toroidal, poloidal], axis=0)
-    packed = parts.reshape(4, ROWS, 2, LANES).transpose(1, 0, 2, 3)
+    tiles = parts.reshape(4, ROWS // 8, 8, 2, LANES).transpose(0, 1, 3, 2, 4)
+    packed = tiles.transpose(1, 3, 0, 2, 4)
     spread = exchange(packed)
     lines = pl.pallas_call(
         plane_kernel,
@@ -203,7 +209,11 @@
         row_kernel,
         out_shape=jax.ShapeDtypeStruct((3, 2, 1, ROWS, COLS), jnp.float32),
         in_specs=[vmem, vmem],
-        out_specs=vmem,
+        out_specs=pl.BlockSpec(memory_space=pl.ANY),
+        scratch_shapes=[
+            pltpu.VMEM((3, 2, ROWS, COLS), jnp.float32),
+            pltpu.SemaphoreType.DMA((3,)),
+        ],
         compiler_params=pltpu.CompilerParams(vmem_limit_bytes=32 * 2**20),
     )(gathered, row_table())
 

time: 65.2 us -> 64.9 us (level)
    concatenate x1 -> x0, other arithmetic: 1.06 us -> none  [local(): parts = jnp.concatenate([toroidal, poloidal], axis=0)]
    reshape x0 -> x1, other arithmetic: none -> 1.06 us  [local(): tiles = parts.reshape(4, ROWS // 8, 8, 2, LANES).transpose(0, 1, 3, 2, 4)]
where the time goes in v5:
time: 64.9 us; the launch traced here: 64.2 us
  blocking collectives  59.6 us (92%)
  Pallas kernels  3.08 us (5%)
  other arithmetic  1.06 us (2%)
    all_to_all x2, blocking collectives, exchange(): lax.all_to_all(chunks, PLANE, 0, 0, axis_index_groups=groups, tiled=True)  59.6 us
    pallas_call x1, Pallas kernels, local(): pl.pallas_call(plane_kernel, out_shape=jax.ShapeDtypeStruct((ROWS * 12, L...  1.78 us
    pallas_call x1, Pallas kernels, local(): pl.pallas_call(row_kernel, out_shape=jax.ShapeDtypeStruct((3, 2, 1, ROWS,...  1.31 us

profile of v5, /device:TPU:8, one launch (start us, length us, event | category | flops | bytes accessed | tf_op | source)
XLA Modules:
  0.0 64.2 jit_solution(6075505986332068707)
XLA Ops:
  0.0 1.1 %maximum_bitcast_fusion = f32[4,16,8,2,128]{4,2,3,1,0:T(8,128)S(1)} fusion(f32[2,1,128,256]{3,2,1,0:T(8,128)} %param.9, f32[2,1,128,256]{3,2,1,0:T(8,128)} %param.8), kind=kLoop, calls=%fused_computation | loop fusion | flops 131072 | bytes 1048576 | tf_op jit(solution)/shard_map/reshape | solution.py:196
  1.1 0.3 copy.10
  1.3 0.0 copy-start
  1.4 0.0 copy-start.2
  1.4 0.0 copy-start.3
  1.4 0.0 copy-start.4
  1.4 0.0 copy-start.5
  1.4 29.1 %all_to_all.10 = f32[128,1,1024]{2,1,0:T(1,128)S(1)} all-to-all(f32[128,1,1024]{2,1,0:T(1,128)S(1)} %bitcast.11), channel_id=1, replica_groups={{190,186,182,188,178,184,180,176,126,122,118,124,114,120,116,112,254,25..., dimensions={0} | all-to-all | bytes 1048576 | tf_op jit(solution)/shard_map/all_to_all | solution.py:189
  30.6 0.0 copy-done
  30.6 0.0 copy-done.2
  30.6 0.0 copy-done.3
  30.6 0.0 copy-done.4
  30.6 0.0 copy-done.5
  30.6 1.8 %shard_map.82 = f32[1536,128]{1,0:T(8,128)S(1)} custom-call(f32[1024,128]{1,0:T(8,128)S(1)} %bitcast.10, bf16[2,256,512]{2,1,0:T(8,128)(2,1)S(1)} %copy-done, bf16[512,256]{1,0:T(8,128)(2,1)S(1)} %copy-done.2, f32[2,16,128]{2,1,0:T(8,128)S(1)} %copy-done.4, f32[16,128]{1,0:T(8,128)S(1)} %copy-done.5, f32[2,128,128]{2,1,0:T(8,128)S(1)} %copy-done.3), custom_call_target="tpu_custom_call" | custom-call | tf_op jit(solution)/shard_map/pallas_call | solution.py:199
  32.4 0.0 copy-start.1
  32.4 30.5 %all_to_all.11 = f32[128,1,1536]{2,1,0:T(1,128)S(1)} all-to-all(f32[128,1,1536]{2,1,0:T(1,128)S(1)} %bitcast.9), channel_id=1, replica_groups={{190,186,182,188,178,184,180,176,126,122,118,124,114,120,116,112,254,25..., dimensions={0} | all-to-all | bytes 1572864 | tf_op jit(solution)/shard_map/all_to_all | solution.py:189
  62.9 0.0 copy-done.1
  62.9 1.3 %shard_map.83 = f32[3,2,1,128,256]{4,3,2,1,0:T(8,128)} custom-call(f32[1536,128]{1,0:T(8,128)S(1)} %bitcast.8, bf16[256,512]{1,0:T(8,128)(2,1)S(1)} %copy-done.1), custom_call_target="tpu_custom_call" | custom-call | tf_op jit(solution)/shard_map/pallas_call | solution.py:208
Async XLA Ops:
  1.3 29.2 %copy-start = (bf16[2,256,512]{2,1,0:T(8,128)(2,1)S(1)}, bf16[2,256,512]{2,1,0:T(8,128)(2,1)}, u32[]{:S(2)}) copy-start(bf16[2,256,512]{2,1,0:T(8,128)(2,1)} %constant.12.clone.outer_ref) | copy-start | bytes 1572868
  1.4 29.2 %copy-start.2 = (bf16[512,256]{1,0:T(8,128)(2,1)S(1)}, bf16[512,256]{1,0:T(8,128)(2,1)}, u32[]{:S(2)}) copy-start(bf16[512,256]{1,0:T(8,128)(2,1)} %constant.13.clone.lane_ref) | copy-start | bytes 786436
  1.4 29.2 %copy-start.3 = (f32[2,128,128]{2,1,0:T(8,128)S(1)}, f32[2,128,128]{2,1,0:T(8,128)}, u32[]{:S(2)}) copy-start(f32[2,128,128]{2,1,0:T(8,128)} %constant.16.clone.wave_ref) | copy-start | bytes 393220
  1.4 29.2 %copy-start.4 = (f32[2,16,128]{2,1,0:T(8,128)S(1)}, f32[2,16,128]{2,1,0:T(8,128)}, u32[]{:S(2)}) copy-start(f32[2,16,128]{2,1,0:T(8,128)} %constant.14.clone.twist_ref) | copy-start | bytes 49156
  1.4 29.2 %copy-start.5 = (f32[16,128]{1,0:T(8,128)S(1)}, f32[16,128]{1,0:T(8,128)}, u32[]{:S(2)}) copy-start(f32[16,128]{1,0:T(8,128)} %constant.15.clone.turn_ref) | copy-start | bytes 24580
  32.4 30.5 %copy-start.1 = (bf16[256,512]{1,0:T(8,128)(2,1)S(1)}, bf16[256,512]{1,0:T(8,128)(2,1)}, u32[]{:S(2)}) copy-start(bf16[256,512]{1,0:T(8,128)(2,1)} %constant.17.clone.table_ref) | copy-start | bytes 786436

commit v6 on v5

--- a/solution.py
+++ b/solution.py
@@ -18,7 +18,7 @@
 COLS = N // GY
 LANES = 128
 PLANE = ("gx", "gy", "gz")
-GX_ORDER = [11, 7, 15, 6, 13, 5, 9, 4, 10, 3, 12, 2, 8, 1, 14, 0]
+GX_ORDER = [8, 1, 12, 5, 15, 7, 14, 4, 13, 2, 10, 3, 9, 0, 11, 6]
 GY_ORDER = [7, 5, 3, 6, 1, 4, 2, 0]
 ORDER = [gx * GY + gy for gx in GX_ORDER for gy in GY_ORDER]
 

time: 64.9 us -> 65 us (level)
  no operation moved by 1% of the time
where the time goes in v6:
time: 65 us; the launch traced here: 64.7 us
  blocking collectives  60.2 us (93%)
  Pallas kernels  3.08 us (5%)
  other arithmetic  1.06 us (2%)
    all_to_all x2, blocking collectives, exchange(): lax.all_to_all(chunks, PLANE, 0, 0, axis_index_groups=groups, tiled=True)  60.2 us
    pallas_call x1, Pallas kernels, local(): pl.pallas_call(plane_kernel, out_shape=jax.ShapeDtypeStruct((ROWS * 12, L...  1.78 us
    pallas_call x1, Pallas kernels, local(): pl.pallas_call(row_kernel, out_shape=jax.ShapeDtypeStruct((3, 2, 1, ROWS,...  1.3 us

profile of v6, /device:TPU:8, one launch (start us, length us, event | category | flops | bytes accessed | tf_op | source)
XLA Modules:
  0.0 64.7 jit_solution(12963568762760236089)
XLA Ops:
  0.0 1.1 %maximum_bitcast_fusion = f32[4,16,8,2,128]{4,2,3,1,0:T(8,128)S(1)} fusion(f32[2,1,128,256]{3,2,1,0:T(8,128)} %param.9, f32[2,1,128,256]{3,2,1,0:T(8,128)} %param.8), kind=kLoop, calls=%fused_computation | loop fusion | flops 131072 | bytes 1048576 | tf_op jit(solution)/shard_map/reshape | solution.py:196
  1.1 0.3 copy.10
  1.3 0.0 copy-start
  1.4 0.0 copy-start.2
  1.4 0.0 copy-start.3
  1.4 0.0 copy-start.4
  1.4 0.0 copy-start.5
  1.4 30.0 %all_to_all.10 = f32[128,1,1024]{2,1,0:T(1,128)S(1)} all-to-all(f32[128,1,1024]{2,1,0:T(1,128)S(1)} %bitcast.11), channel_id=1, replica_groups={{142,138,134,140,130,136,132,128,30,26,22,28,18,24,20,16,206,202,198,20..., dimensions={0} | all-to-all | bytes 1048576 | tf_op jit(solution)/shard_map/all_to_all | solution.py:189
  31.5 0.0 copy-done
  31.5 0.0 copy-done.2
  31.5 0.0 copy-done.3
  31.5 0.0 copy-done.4
  31.5 0.0 copy-done.5
  31.5 1.8 %shard_map.82 = f32[1536,128]{1,0:T(8,128)S(1)} custom-call(f32[1024,128]{1,0:T(8,128)S(1)} %bitcast.10, bf16[2,256,512]{2,1,0:T(8,128)(2,1)S(1)} %copy-done, bf16[512,256]{1,0:T(8,128)(2,1)S(1)} %copy-done.2, f32[2,16,128]{2,1,0:T(8,128)S(1)} %copy-done.4, f32[16,128]{1,0:T(8,128)S(1)} %copy-done.5, f32[2,128,128]{2,1,0:T(8,128)S(1)} %copy-done.3), custom_call_target="tpu_custom_call" | custom-call | tf_op jit(solution)/shard_map/pallas_call | solution.py:199
  33.3 0.0 copy-start.1
  33.3 30.1 %all_to_all.11 = f32[128,1,1536]{2,1,0:T(1,128)S(1)} all-to-all(f32[128,1,1536]{2,1,0:T(1,128)S(1)} %bitcast.9), channel_id=1, replica_groups={{142,138,134,140,130,136,132,128,30,26,22,28,18,24,20,16,206,202,198,20..., dimensions={0} | all-to-all | bytes 1572864 | tf_op jit(solution)/shard_map/all_to_all | solution.py:189
  63.4 0.0 copy-done.1
  63.4 1.3 %shard_map.83 = f32[3,2,1,128,256]{4,3,2,1,0:T(8,128)} custom-call(f32[1536,128]{1,0:T(8,128)S(1)} %bitcast.8, bf16[256,512]{1,0:T(8,128)(2,1)S(1)} %copy-done.1), custom_call_target="tpu_custom_call" | custom-call | tf_op jit(solution)/shard_map/pallas_call | solution.py:208
Async XLA Ops:
  1.3 30.1 %copy-start = (bf16[2,256,512]{2,1,0:T(8,128)(2,1)S(1)}, bf16[2,256,512]{2,1,0:T(8,128)(2,1)}, u32[]{:S(2)}) copy-start(bf16[2,256,512]{2,1,0:T(8,128)(2,1)} %constant.12.clone.outer_ref) | copy-start | bytes 1572868
  1.4 30.1 %copy-start.2 = (bf16[512,256]{1,0:T(8,128)(2,1)S(1)}, bf16[512,256]{1,0:T(8,128)(2,1)}, u32[]{:S(2)}) copy-start(bf16[512,256]{1,0:T(8,128)(2,1)} %constant.13.clone.lane_ref) | copy-start | bytes 786436
  1.4 30.1 %copy-start.3 = (f32[2,128,128]{2,1,0:T(8,128)S(1)}, f32[2,128,128]{2,1,0:T(8,128)}, u32[]{:S(2)}) copy-start(f32[2,128,128]{2,1,0:T(8,128)} %constant.16.clone.wave_ref) | copy-start | bytes 393220
  1.4 30.1 %copy-start.4 = (f32[2,16,128]{2,1,0:T(8,128)S(1)}, f32[2,16,128]{2,1,0:T(8,128)}, u32[]{:S(2)}) copy-start(f32[2,16,128]{2,1,0:T(8,128)} %constant.14.clone.twist_ref) | copy-start | bytes 49156
  1.4 30.1 %copy-start.5 = (f32[16,128]{1,0:T(8,128)S(1)}, f32[16,128]{1,0:T(8,128)}, u32[]{:S(2)}) copy-start(f32[16,128]{1,0:T(8,128)} %constant.15.clone.turn_ref) | copy-start | bytes 24580
  33.3 30.1 %copy-start.1 = (bf16[256,512]{1,0:T(8,128)(2,1)S(1)}, bf16[256,512]{1,0:T(8,128)(2,1)}, u32[]{:S(2)}) copy-start(bf16[256,512]{1,0:T(8,128)(2,1)} %constant.17.clone.table_ref) | copy-start | bytes 786436

commit v7 on v5

--- a/solution.py
+++ b/solution.py
@@ -175,10 +175,11 @@
         ]
         high, low = halves(jnp.concatenate(parts, axis=0))
         value = table_times(table_ref[...], high, low)
-        value_ref[comp, 0] = value[:ROWS]
-        value_ref[comp, 1] = value[ROWS:]
-        copies.append(pltpu.make_async_copy(value_ref.at[comp], out_ref.at[comp, :, 0], sems.at[comp]))
-        copies[-1].start()
+        for imag in range(2):
+            value_ref[comp, imag] = value[imag * ROWS : (imag + 1) * ROWS]
+            source, target = value_ref.at[comp, imag], out_ref.at[comp, imag, 0]
+            copies.append(pltpu.make_async_copy(source, target, sems.at[comp * 2 + imag]))
+            copies[-1].start()
     for copy in copies:
         copy.wait()
 
@@ -212,7 +213,7 @@
         out_specs=pl.BlockSpec(memory_space=pl.ANY),
         scratch_shapes=[
             pltpu.VMEM((3, 2, ROWS, COLS), jnp.float32),
-            pltpu.SemaphoreType.DMA((3,)),
+            pltpu.SemaphoreType.DMA((6,)),
         ],
         compiler_params=pltpu.CompilerParams(vmem_limit_bytes=32 * 2**20),
     )(gathered, row_table())

time: 64.9 us -> 64.9 us (level)
  no operation moved by 1% of the time
where the time goes in v7:
time: 64.9 us; the launch traced here: 64.2 us
  blocking collectives  59.6 us (92%)
  Pallas kernels  3.07 us (5%)
  other arithmetic  1.06 us (2%)
    all_to_all x2, blocking collectives, exchange(): lax.all_to_all(chunks, PLANE, 0, 0, axis_index_groups=groups, tiled=True)  59.6 us
    pallas_call x1, Pallas kernels, local(): pl.pallas_call(plane_kernel, out_shape=jax.ShapeDtypeStruct((ROWS * 12, L...  1.78 us

profile of v7, /device:TPU:8, one launch (start us, length us, event | category | flops | bytes accessed | tf_op | source)
XLA Modules:
  0.0 64.2 jit_solution(5476332808094975982)
XLA Ops:
  0.0 1.1 %maximum_bitcast_fusion = f32[4,16,8,2,128]{4,2,3,1,0:T(8,128)S(1)} fusion(f32[2,1,128,256]{3,2,1,0:T(8,128)} %param.9, f32[2,1,128,256]{3,2,1,0:T(8,128)} %param.8), kind=kLoop, calls=%fused_computation | loop fusion | flops 131072 | bytes 1048576 | tf_op jit(solution)/shard_map/reshape | solution.py:197
  1.1 0.3 copy.10
  1.3 0.0 copy-start
  1.4 0.0 copy-start.2
  1.4 0.0 copy-start.3
  1.4 0.0 copy-start.4
  1.4 0.0 copy-start.5
  1.4 29.1 %all_to_all.10 = f32[128,1,1024]{2,1,0:T(1,128)S(1)} all-to-all(f32[128,1,1024]{2,1,0:T(1,128)S(1)} %bitcast.11), channel_id=1, replica_groups={{190,186,182,188,178,184,180,176,126,122,118,124,114,120,116,112,254,25..., dimensions={0} | all-to-all | bytes 1048576 | tf_op jit(solution)/shard_map/all_to_all | solution.py:190
  30.6 0.0 copy-done
  30.6 0.0 copy-done.2
  30.6 0.0 copy-done.3
  30.6 0.0 copy-done.4
  30.6 0.0 copy-done.5
  30.6 1.8 %shard_map.82 = f32[1536,128]{1,0:T(8,128)S(1)} custom-call(f32[1024,128]{1,0:T(8,128)S(1)} %bitcast.10, bf16[2,256,512]{2,1,0:T(8,128)(2,1)S(1)} %copy-done, bf16[512,256]{1,0:T(8,128)(2,1)S(1)} %copy-done.2, f32[2,16,128]{2,1,0:T(8,128)S(1)} %copy-done.4, f32[16,128]{1,0:T(8,128)S(1)} %copy-done.5, f32[2,128,128]{2,1,0:T(8,128)S(1)} %copy-done.3), custom_call_target="tpu_custom_call" | custom-call | tf_op jit(solution)/shard_map/pallas_call | solution.py:200
  32.4 0.0 copy-start.1
  32.4 30.5 %all_to_all.11 = f32[128,1,1536]{2,1,0:T(1,128)S(1)} all-to-all(f32[128,1,1536]{2,1,0:T(1,128)S(1)} %bitcast.9), channel_id=1, replica_groups={{190,186,182,188,178,184,180,176,126,122,118,124,114,120,116,112,254,25..., dimensions={0} | all-to-all | bytes 1572864 | tf_op jit(solution)/shard_map/all_to_all | solution.py:190
  62.9 0.0 copy-done.1
  62.9 1.3 %shard_map.83 = f32[3,2,1,128,256]{4,3,2,1,0:T(8,128)} custom-call(f32[1536,128]{1,0:T(8,128)S(1)} %bitcast.8, bf16[256,512]{1,0:T(8,128)(2,1)S(1)} %copy-done.1), custom_call_target="tpu_custom_call" | custom-call | tf_op jit(solution)/shard_map/pallas_call | solution.py:209
Async XLA Ops:
  1.3 29.2 %copy-start = (bf16[2,256,512]{2,1,0:T(8,128)(2,1)S(1)}, bf16[2,256,512]{2,1,0:T(8,128)(2,1)}, u32[]{:S(2)}) copy-start(bf16[2,256,512]{2,1,0:T(8,128)(2,1)} %constant.12.clone.outer_ref) | copy-start | bytes 1572868
  1.4 29.2 %copy-start.2 = (bf16[512,256]{1,0:T(8,128)(2,1)S(1)}, bf16[512,256]{1,0:T(8,128)(2,1)}, u32[]{:S(2)}) copy-start(bf16[512,256]{1,0:T(8,128)(2,1)} %constant.13.clone.lane_ref) | copy-start | bytes 786436
  1.4 29.2 %copy-start.3 = (f32[2,128,128]{2,1,0:T(8,128)S(1)}, f32[2,128,128]{2,1,0:T(8,128)}, u32[]{:S(2)}) copy-start(f32[2,128,128]{2,1,0:T(8,128)} %constant.16.clone.wave_ref) | copy-start | bytes 393220
  1.4 29.2 %copy-start.4 = (f32[2,16,128]{2,1,0:T(8,128)S(1)}, f32[2,16,128]{2,1,0:T(8,128)}, u32[]{:S(2)}) copy-start(f32[2,16,128]{2,1,0:T(8,128)} %constant.14.clone.twist_ref) | copy-start | bytes 49156
  1.4 29.2 %copy-start.5 = (f32[16,128]{1,0:T(8,128)S(1)}, f32[16,128]{1,0:T(8,128)}, u32[]{:S(2)}) copy-start(f32[16,128]{1,0:T(8,128)} %constant.15.clone.turn_ref) | copy-start | bytes 24580
  32.4 30.5 %copy-start.1 = (bf16[256,512]{1,0:T(8,128)(2,1)S(1)}, bf16[256,512]{1,0:T(8,128)(2,1)}, u32[]{:S(2)}) copy-start(bf16[256,512]{1,0:T(8,128)(2,1)} %constant.17.clone.table_ref) | copy-start | bytes 786436
